TPU v7x, 32 devices: a whole 2x2x4 slice. The times are simulated.
32 devices in a mesh: groups: 2 (over y), rep: 4 (over x, core), tp: 4 (over z).
Axes of the slice: x: 2, y: 2, z: 4, core: 2. Of those that a mesh axis runs over, the one named last changes fastest.
Arguments:
- queries: bfloat16 [2048, 4096], P(('groups', 'rep'), 'tp'), parts along dimension 0, may hold values from -4.5 to 4.5
- keys: bfloat16 [16, 3200, 4, 128], P(('groups', 'rep'), 'tp'), parts along dimension 0, may hold values from -4.5 to 4.5
- values: bfloat16 [16, 3200, 4, 128], P(('groups', 'rep'), 'tp'), parts along dimension 0, may hold values from -24 to 24
- lengths: int32 [16], P(('groups', 'rep')), parts along dimension 0, may hold values from 1 to 128, as said below
- offsets: int32 [16], P(('groups', 'rep')), parts along dimension 0, may hold values from 0 to 3072, as said below
- tenants: int32 [16], P(('groups', 'rep')), parts along dimension 0, may hold values from 0 to 127
- tenant_storage_rows: int32 [128], replicated, may hold values from 0 to 127, each once
- output_weight: bfloat16 [4096, 5120], P(None, 'tp'), may hold values from -0.09375 to 0.09375
- adapter_down_factors: bfloat16 [128, 64, 4096], P(None, 'rep', 'tp'), may hold values from -0.09375 to 0.09375
- adapter_up_factors: bfloat16 [128, 64, 5120], P(None, 'rep', 'tp'), may hold values from -0.75 to 0.75
Outputs:
- mixed: bfloat16 [2048, 5120], P(('groups', 'rep'), 'tp'), parts along dimension 0
There are 2 independent parts, one for each index of `groups`. A program takes and returns all parts, laid end to end along the dimension named above; an argument that names none is the same for every part. Nothing has to cross between parts.
Inputs may be any that keep to these rules, and one draw needn't show every extreme that they name: `lengths`: some block has exactly 128 new rows and some block exactly one. offsets[b] + lengths[b] <= 3200 for every block; some block reaches 3200 with 128 new rows, and some block starts at 0. `tenants`: several blocks may share a tenant. `tenant_storage_rows`: every storage row once.
All inputs are finite; a program needn't handle non-finite values.
Results may differ from a plain program's by a relative error of at most 0.0061.
Values may be sent and summed in bfloat16 or wider, within the bound.
A program may use at most 128 MiB of HBM per device.

v0:
```python
import math

import jax
import jax.numpy as jnp
from jax import lax
from jax.sharding import PartitionSpec as P


def attend(queries, head_keys, head_values, lengths, offsets, head_dim):
    blocks_per_device = lengths.shape[0]
    block_rows = queries.shape[0] // blocks_per_device
    local_heads = queries.shape[1] // head_dim
    context = head_keys.shape[1]
    score_scale = 1.0 / math.sqrt(head_dim)
    blocks_of_queries = queries.reshape(blocks_per_device, block_rows, local_heads, head_dim)
    scores = (
        jnp.einsum(
            "xovs,xts->xvot", blocks_of_queries, head_keys, preferred_element_type=jnp.float32
        )
        * score_scale
    )
    row_ids = jnp.arange(block_rows, dtype=jnp.int32)
    position_ids = jnp.arange(context, dtype=jnp.int32)
    visible = position_ids[None, None, :] <= offsets[:, None, None] + row_ids[None, :, None]
    scores = jnp.where(visible[:, None], scores, -1e30)
    top_score = jnp.max(scores, axis=-1, keepdims=True)
    weights = jnp.exp(scores - top_score)
    probabilities = (weights / jnp.sum(weights, axis=-1, keepdims=True)).astype(jnp.bfloat16)
    projected_output = jnp.einsum(
        "lzug,lgy->luzy", probabilities, head_values, preferred_element_type=jnp.float32
    )
    live_rows = row_ids[None, :] < lengths[:, None]
    projected_output = jnp.where(live_rows[:, :, None, None], projected_output, 0.0).astype(
        jnp.bfloat16
    )
    return projected_output.reshape(blocks_per_device * block_rows, local_heads * head_dim)


def on_device(
    queries,
    keys,
    values,
    lengths,
    offsets,
    tenants,
    tenant_storage_rows,
    output_weight,
    adapter_down_factors,
    adapter_up_factors,
):
    tp_count = lax.axis_size("tp")
    repeat_count = lax.axis_size("rep")
    kv_heads = keys.shape[2]
    head_dim = keys.shape[3]
    blocks_per_device = lengths.shape[0]
    row_count = queries.shape[0]
    block_rows = row_count // blocks_per_device
    local_width = queries.shape[1]
    out_width = output_weight.shape[1]
    copies = tp_count // kv_heads
    sent_keys = jnp.repeat(keys, copies, axis=2)
    sent_values = jnp.repeat(values, copies, axis=2)
    got_keys, got_values = (
        lax.all_to_all(sent_keys, "tp", split_axis=2, concat_axis=1, tiled=True),
        lax.all_to_all(sent_values, "tp", split_axis=2, concat_axis=1, tiled=True),
    )
    head_keys = got_keys[:, :, 0, :]
    head_values = got_values[:, :, 0, :]
    attended = attend(queries, head_keys, head_values, lengths, offsets, head_dim)
    all_tenants = lax.all_gather(tenants, "rep", axis=0, tiled=True)
    catalog = jnp.arange(tenant_storage_rows.shape[0], dtype=jnp.int32)
    storage_slot_rows = jnp.sum(
        jnp.where(all_tenants[:, None] == catalog[None, :], tenant_storage_rows[None, :], 0), axis=1
    )
    selected_down = jnp.take(adapter_down_factors, storage_slot_rows, axis=0)
    selected_up = jnp.take(adapter_up_factors, storage_slot_rows, axis=0)
    selected_down = selected_down.reshape(
        repeat_count,
        blocks_per_device,
        adapter_down_factors.shape[1],
        adapter_down_factors.shape[2],
    )
    selected_up = selected_up.reshape(
        repeat_count, blocks_per_device, adapter_up_factors.shape[1], adapter_up_factors.shape[2]
    )
    down_factor_rows, up_factor_rows = (
        lax.all_to_all(selected_down, "rep", split_axis=0, concat_axis=2, tiled=True),
        lax.all_to_all(selected_up, "rep", split_axis=0, concat_axis=2, tiled=True),
    )
    down_factor_rows = down_factor_rows[0]
    up_factor_rows = up_factor_rows[0]
    attended_blocks = attended.reshape(blocks_per_device, block_rows, local_width)
    portion_rows = lax.all_gather(attended_blocks, "tp", axis=2, tiled=True)
    piece_down = lax.all_gather(down_factor_rows, "tp", axis=2, tiled=True)
    base_next = jnp.einsum(
        "kvz,zy->kvy", portion_rows, output_weight, preferred_element_type=jnp.float32
    )
    low_next = jnp.einsum(
        "bqw,brw->bqr", portion_rows, piece_down, preferred_element_type=jnp.float32
    )
    rank_product = low_next.astype(jnp.bfloat16)
    adapter_delta = jnp.einsum(
        "pmx,pxy->pmy", rank_product, up_factor_rows, preferred_element_type=jnp.float32
    )
    mixed = (base_next + adapter_delta).astype(jnp.bfloat16)
    return mixed.reshape(row_count, out_width)


def solution(mesh):
    return jax.shard_map(
        on_device,
        mesh=mesh,
        in_specs=(
            P(("groups", "rep"), "tp"),
            P(("groups", "rep"), "tp", None, None),
            P(("groups", "rep"), "tp", None, None),
            P(("groups", "rep")),
            P(("groups", "rep")),
            P(("groups", "rep")),
            P(),
            P(None, "tp"),
            P(None, "rep", "tp"),
            P(None, "rep", "tp"),
        ),
        out_specs=P(("groups", "rep"), "tp"),
        check_vma=False,
    )
```

profile of v0, /device:TPU:0, one launch (start us, length us, event | category | flops | bytes accessed | tf_op | source)
XLA Modules:
  0.0 190.4 jit_solution(17551706001280996709)
XLA Ops:
  6.5 2.8 %copy.46 = bf16[2,800,4,128]{3,1,0,2:T(8,128)(2,1)} copy(bf16[2,800,4,128]{3,2,1,0:T(4,128)(2,1)} %param.11) | data formatting | bytes 3276800 | tf_op args[1]
  9.4 6.4 %all-to-all-start = ((bf16[2,800,4,128]{3,1,0,2:T(8,128)(2,1)}), bf16[2,800,4,128]{3,1,0,2:T(8,128)(2,1)S(1)}, u32[]{:S(2)}, u32[]{:S(2)}) async-start(bf16[2,800,4,128]{3,1,0,2:T(8,128)(2,1)} %copy.46), calls=%async_computation | async-start | bytes 3276800 | tf_op jit(solution)/shard_map/all_to_all | solution.py:64
  15.8 0.0 copy-done.1
  15.8 1.4 copy.49
  17.2 0.0 copy-done.2
  17.2 0.9 copy.61
  18.1 0.0 copy-done.3
  18.1 0.1 iota_add_fusion
  18.2 1.5 iota_compare_fusion
  19.6 34.5 %all-to-all-done = bf16[2,800,4,128]{3,1,0,2:T(8,128)(2,1)S(1)} async-done(((bf16[2,800,4,128]{3,1,0,2:T(8,128)(2,1)}), bf16[2,800,4,128]{3,1,0,2:T(8,128)(2,1)S(1)}, u32[]{:S(2)}, u32[]{:S(2)}) %all-to-all-start) | async-done | bytes 1638432 | tf_op jit(solution)/shard_map/all_to_all | solution.py:64
  54.2 3.6 %all-to-all-start.1 = ((bf16[2,800,4,128]{3,1,0,2:T(8,128)(2,1)}), bf16[2,800,4,128]{3,1,0,2:T(8,128)(2,1)S(1)}, u32[]{:S(2)}, u32[]{:S(2)}) async-start(bf16[2,800,4,128]{3,1,0,2:T(8,128)(2,1)} %copy.49), calls=%async_computation.1 | async-start | bytes 3276800 | tf_op jit(solution)/shard_map/all_to_all | solution.py:65
  57.8 0.0 all-gather.3.cloned.1.call-start
  57.8 0.0 copy-done.4
  57.8 0.1 iota_compare_fusion.2
  57.9 1.3 copy.47
  59.2 14.8 %fusion.23 = (f32[2,8,128]{2,1,0:T(8,128)S(1)}, f32[2,8,128,3200]{2,3,1,0:T(8,128)}) fusion(pred[2,128,3200]{1,2,0:T(8,128)(4,1)} %iota_compare_fusion, bf16[2,3200,128,1]{2,1,3,0:T(8,128)(2,1)} %bitcast.61, bf16[2,128,8,128]{3,2,1,0:T(8,128)(2,1)} %bitcast.70), kind=kOutput, calls=%fused_computation.36 | convolution fusion | flops 1703939200 | bytes 29204480 | tf_op jit(solution)/shard_map/sub | solution.py:27
  74.0 21.6 %all-to-all-done.1 = bf16[2,800,4,128]{3,1,0,2:T(8,128)(2,1)S(1)} async-done(((bf16[2,800,4,128]{3,1,0,2:T(8,128)(2,1)}), bf16[2,800,4,128]{3,1,0,2:T(8,128)(2,1)S(1)}, u32[]{:S(2)}, u32[]{:S(2)}) %all-to-all-start.1) | async-done | bytes 1638432 | tf_op jit(solution)/shard_map/all_to_all | solution.py:65
  95.6 0.1 copy.50
  95.7 0.0 copy-start.7
  95.7 0.0 copy-start.5
  95.7 0.0 copy-start.6
  95.7 9.9 %fusion.12 = bf16[2,8,128,128]{2,3,1,0:T(8,128)(2,1)S(1)} fusion(bf16[2,3200,128,1]{2,1,3,0:T(8,128)(2,1)S(1)} %bitcast.62, f32[2,8,128,3200]{2,3,1,0:T(8,128)} %get-tuple-element.6, f32[2,8,128]{2,1,0:T(8,128)S(1)} %get-tuple-element.5, pred[2,128]{1,0:T(4,128)(4,1)S(1)} %iota_compare_fusion.2), kind=kOutput, calls=%fused_computation.18 | convolution fusion | flops 1691353088 | bytes 28385536 | tf_op jit(solution)/shard_map/lzug,lgy->luzy/dot_general | solution.py:29
  105.7 1.0 copy.53
  106.7 0.0 all-gather.3.cloned.1.call-update
  106.7 0.0 copy-done.7
  106.7 0.6 dynamic-slice
  108.0 0.0 copy-done.5
  108.0 0.2 dynamic-update-slice
  108.2 4.9 %all-reduce = s32[8]{0:T(128)S(1)} all-reduce(s32[8]{0:T(128)S(1)} %dynamic-update-slice), channel_id=1, replica_groups=mesh['groups'=2,'rep'=4,'tp'=4] {'rep'}, use_global_device_ids=true, to_apply=%add | all-reduce | flops 8 | bytes 64
  113.1 0.0 copy-done.6
  113.1 0.2 select_reduce_fusion
  113.3 0.1 reduce_sum.24
  113.4 2.9 %gather_fusion = bf16[8,16,1024]{2,1,0:T(8,128)(2,1)S(1)} fusion(bf16[128,16,1024]{2,1,0:T(8,128)(2,1)} %param.18, s32[1024]{0:T(1024)S(1)} %pad_clamp_fusion), kind=kCustom, calls=%fused_computation | custom fusion | bytes 524320 | tf_op jit(solution)/shard_map/jit(_take)/gather | solution.py:75
  116.4 0.8 broadcast_select_fusion.1
  117.2 3.4 %all-to-all-start.2 = ((bf16[4,2,16,1024]{3,2,1,0:T(8,128)(2,1)}), bf16[4,2,16,1024]{3,2,1,0:T(8,128)(2,1)S(1)}, u32[]{:S(2)}, u32[]{:S(2)}) async-start(bf16[4,2,16,1024]{3,2,1,0:T(8,128)(2,1)} %broadcast_select_fusion.1), calls=%async_computation.2 | async-start | bytes 524288 | tf_op jit(solution)/shard_map/all_to_all | solution.py:87
  120.6 0.0 all-gather.5.cloned.1.call-start
  120.6 3.1 %gather_fusion.1 = bf16[8,16,1280]{2,1,0:T(8,128)(2,1)S(1)} fusion(bf16[128,16,1280]{2,1,0:T(8,128)(2,1)} %param.19, s32[1024]{0:T(1024)S(1)} %pad_clamp_fusion), kind=kCustom, calls=%fused_computation.1 | custom fusion | bytes 655392 | tf_op jit(solution)/shard_map/jit(_take)/gather | solution.py:76
  123.7 2.9 %all-to-all-done.2 = bf16[4,2,16,1024]{3,2,1,0:T(8,128)(2,1)S(1)} async-done(((bf16[4,2,16,1024]{3,2,1,0:T(8,128)(2,1)}), bf16[4,2,16,1024]{3,2,1,0:T(8,128)(2,1)S(1)}, u32[]{:S(2)}, u32[]{:S(2)}) %all-to-all-start.2) | async-done | bytes 262176 | tf_op jit(solution)/shard_map/all_to_all | solution.py:87
  126.6 0.7 copy.54
  127.3 0.0 all-gather.5.cloned.1.call-update
  127.3 0.1 broadcast_select_fusion
  127.5 9.1 %all_to_all.60 = bf16[4,2,16,1280]{3,2,1,0:T(8,128)(2,1)S(1)} all-to-all(bf16[4,2,16,1280]{3,2,1,0:T(8,128)(2,1)S(1)} %broadcast_select_fusion), channel_id=1, replica_groups=mesh['groups'=2,'rep'=4,'tp'=4] {'rep'}, dimensions={0} | all-to-all | bytes 655360 | tf_op jit(solution)/shard_map/all_to_all | solution.py:88
  136.6 0.7 copy.55
  137.3 14.6 %all-gather.3.cloned.1.call-done = bf16[2,128,4096]{2,1,0:T(8,128)(2,1)} async-done(((bf16[2,128,1024]{2,1,0:T(8,128)(2,1)}), bf16[2,128,4096]{2,1,0:T(8,128)(2,1)}) %all-gather.3.cloned.1.call-update) | async-done | bytes 2097168 | tf_op jit(solution)/shard_map/all_gather | solution.py:93
  151.9 7.6 %fusion.6 = f32[2,128,1280]{2,1,0:T(8,128)S(1)} fusion(bf16[2,128,4096]{2,1,0:T(8,128)(2,1)} %all-gather.3.cloned.1.call-done, bf16[4096,1280]{1,0:T(8,128)(2,1)} %param.17), kind=kOutput, calls=%fused_computation.11 | convolution fusion | flops 2684354560 | bytes 13893632 | tf_op jit(solution)/shard_map/kvz,zy->kvy/dot_general | solution.py:95
  159.6 20.6 %all-gather.5.cloned.1.call-done = bf16[2,64,4096]{2,1,0:T(8,128)(2,1)} async-done(((bf16[2,64,1024]{2,1,0:T(8,128)(2,1)}), bf16[2,64,4096]{2,1,0:T(8,128)(2,1)}) %all-gather.5.cloned.1.call-update) | async-done | bytes 1048592 | tf_op jit(solution)/shard_map/all_gather | solution.py:94
  180.2 0.0 copy-done
  180.2 3.3 %fusion.10 = bf16[2,128,1280]{2,1,0:T(8,128)(2,1)} fusion(f32[2,128,1280]{2,1,0:T(8,128)S(1)} %fusion.6, bf16[2,64,1280]{2,1,0:T(8,128)(2,1)} %bitcast.65, bf16[2,128,4096]{2,1,0:T(8,128)(2,1)S(1)} %copy-done, bf16[2,64,4096]{2,1,0:T(8,128)(2,1)} %all-gather.5.cloned.1.call-done), kind=kOutput, calls=%fused_computation.16 | convolution fusion | flops 176832512 | bytes 5439488 | tf_op jit(solution)/shard_map/pmx,pxy->pmy/dot_general | solution.py:102
  (9 shorter events, 0.0 us)
Async XLA Ops:
  9.4 6.5 %copy-start.1 = (bf16[2,800,4,128]{3,2,1,0:T(4,128)(2,1)S(1)}, bf16[2,800,4,128]{3,2,1,0:T(4,128)(2,1)}, u32[]{:S(2)}) copy-start(bf16[2,800,4,128]{3,2,1,0:T(4,128)(2,1)} %param.12) | copy-start | bytes 4915204
  9.4 44.8 %all-to-all-start = ((bf16[2,800,4,128]{3,1,0,2:T(8,128)(2,1)}), bf16[2,800,4,128]{3,1,0,2:T(8,128)(2,1)S(1)}, u32[]{:S(2)}, u32[]{:S(2)}) async-start(bf16[2,800,4,128]{3,1,0,2:T(8,128)(2,1)} %copy.46), calls=%async_computation | async-start | bytes 3276800 | tf_op jit(solution)/shard_map/all_to_all | solution.py:64
  15.8 1.4 copy-start.2
  15.8 2.3 %copy-start.3 = (s32[2]{0:T(128)S(1)}, s32[2]{0:T(128)}, u32[]{:S(2)}) copy-start(s32[2]{0:T(128)} %param.14) | copy-start | bytes 28
  18.1 39.7 %copy-start.4 = (s32[2]{0:T(128)S(1)}, s32[2]{0:T(128)}, u32[]{:S(2)}) copy-start(s32[2]{0:T(128)} %param.13) | copy-start | bytes 28
  54.2 41.4 %all-to-all-start.1 = ((bf16[2,800,4,128]{3,1,0,2:T(8,128)(2,1)}), bf16[2,800,4,128]{3,1,0,2:T(8,128)(2,1)S(1)}, u32[]{:S(2)}, u32[]{:S(2)}) async-start(bf16[2,800,4,128]{3,1,0,2:T(8,128)(2,1)} %copy.49), calls=%async_computation.1 | async-start | bytes 3276800 | tf_op jit(solution)/shard_map/all_to_all | solution.py:65
  57.8 94.2 %all-gather.3.cloned.1.call-start = ((), (), s32[]{:S(2)}) async-start(), calls=%async_computation.4 | async-start | bytes 2621440 | tf_op jit(solution)/shard_map/all_gather | solution.py:93
  95.7 11.0 %copy-start.7 = (u32[32]{0:T(128)S(1)}, u32[32]{0:T(128)}, u32[]{:S(2)}) copy-start(u32[32]{0:T(128)} %constant.44) | copy-start | bytes 388
  95.7 12.3 %copy-start.5 = (s32[2]{0:T(128)S(1)}, s32[2]{0:T(128)}, u32[]{:S(2)}) copy-start(s32[2]{0:T(128)} %param.15) | copy-start | bytes 28
  95.7 17.4 %copy-start.6 = (s32[128]{0:T(128)S(1)}, s32[128]{0:T(128)}, u32[]{:S(2)}) copy-start(s32[128]{0:T(128)} %param.16) | copy-start | bytes 1540
  117.2 9.4 %all-to-all-start.2 = ((bf16[4,2,16,1024]{3,2,1,0:T(8,128)(2,1)}), bf16[4,2,16,1024]{3,2,1,0:T(8,128)(2,1)S(1)}, u32[]{:S(2)}, u32[]{:S(2)}) async-start(bf16[4,2,16,1024]{3,2,1,0:T(8,128)(2,1)} %broadcast_select_fusion.1), calls=%async_computation.2 | async-start | bytes 524288 | tf_op jit(solution)/shard_map/all_to_all | solution.py:87
  120.6 59.6 %all-gather.5.cloned.1.call-start = ((), (), s32[]{:S(2)}) async-start(), calls=%async_computation.5 | async-start | bytes 1310720 | tf_op jit(solution)/shard_map/all_gather | solution.py:94
  151.9 28.3 %copy-start = (bf16[2,128,4096]{2,1,0:T(8,128)(2,1)S(1)}, bf16[2,128,4096]{2,1,0:T(8,128)(2,1)}, u32[]{:S(2)}) copy-start(bf16[2,128,4096]{2,1,0:T(8,128)(2,1)} %all-gather.3.cloned.1.call-done) | copy-start | bytes 6291460
Sparse Core Ops, SparseCore 0:
  106.8 45.0 all-gather.2
  153.5 26.6 all-gather.4
where the time goes:
time: 191 us; the launch traced here: 190 us
  waiting for transfers between devices  94.3 us (49%)
  matrix products  35.7 us (19%)
  local copies, waits for them, and re-layouts  16 us (8%)
  between operations  14.2 us (7%)
  blocking collectives  14 us (7%)
  starting transfers between devices  13.5 us (7%)
  other arithmetic  2.69 us (1%)
    all_to_all x1, waiting for transfers between devices, on_device(): lax.all_to_all(sent_keys, 'tp', split_axis=2, concat_axis=1, tiled=True)  34.5 us
    all_to_all x1, waiting for transfers between devices, on_device(): lax.all_to_all(sent_values, 'tp', split_axis=2, concat_axis=1, tiled=True)  21.6 us
    all_gather x1, waiting for transfers between devices, on_device(): piece_down = lax.all_gather(down_factor_rows, 'tp', axis=2, tiled=True)  20.6 us
    sub x1, matrix products, attend(): weights = jnp.exp(scores - top_score)  14.8 us
    all_gather x1, waiting for transfers between devices, on_device(): portion_rows = lax.all_gather(attended_blocks, 'tp', axis=2, tiled=True)  14.6 us
    dot_general x1, matrix products, attend(): jnp.einsum('lzug,lgy->luzy', probabilities, head_values, preferred_elemen...  9.92 us
    all_to_all x1, blocking collectives, on_device(): lax.all_to_all(selected_up, 'rep', split_axis=0, concat_axis=2, tiled=True)  9.11 us
    dot_general x1, matrix products, on_device(): jnp.einsum('kvz,zy->kvy', portion_rows, output_weight, preferred_element_...  7.62 us
  transfers between devices with their start and end apart: 5, of which 5 were waited for; matrix products, arithmetic and copies ran while one was open for 20% of the time, Pallas kernels for 0%

commit v1 on v0

v1 whole, which is shorter than its diff:
```python
import functools
import math

import jax
import jax.numpy as jnp
from jax import lax
from jax.experimental import pallas as pl
from jax.experimental.pallas import tpu as pltpu
from jax.sharding import PartitionSpec as P

MESH = pl.DeviceIdType.MESH


def kernel(
    n,
    reps,
    copies,
    chunk,
    kept,
    off_ref,
    len_ref,
    q_ref,
    k_hbm,
    v_hbm,
    w_hbm,
    down_hbm,
    up_hbm,
    o_ref,
    kbuf,
    vbuf,
    probs,
    rows_all,
    low_all,
    dbuf,
    ubuf,
    wbuf,
    kv_send,
    kv_recv,
    own_sem,
    w_sem,
    ad_send,
    ad_recv,
    ad_own,
    row_send,
    row_recv,
    low_send,
    low_recv,
):
    blocks = k_hbm.shape[0]
    padded = k_hbm.shape[1]
    hd = kbuf.shape[-1]
    block_rows = q_ref.shape[0] // blocks
    width = q_ref.shape[1]
    heads = width // hd
    me = lax.axis_index("tp")
    my_rep = lax.axis_index("rep")

    def peer(d):
        return lax.rem(me + d, n)

    def source(d):
        return lax.rem(me + n - d, n)

    def rpeer(d):
        return lax.rem(my_rep + d, reps)

    def rsource(d):
        return lax.rem(my_rep + reps - d, reps)

    barrier = pltpu.get_barrier_semaphore()
    for d in range(1, n):
        pl.semaphore_signal(barrier, inc=1, device_id={"tp": peer(d)}, device_id_type=MESH)
    for d in range(1, reps):
        pl.semaphore_signal(barrier, inc=1, device_id={"rep": rpeer(d)}, device_id_type=MESH)
    pl.semaphore_wait(barrier, n - 1 + reps - 1)

    hbms = (k_hbm, v_hbm)
    bufs = (kbuf, vbuf)

    def columns(t):
        return pl.ds(pl.multiple_of((t // copies) * hd, hd), hd)

    def span(t):
        return pl.ds(pl.multiple_of(t * padded, 16), padded)

    def kv_copy(b, kind, d, slot, to):
        return pltpu.make_async_remote_copy(
            src_ref=hbms[kind].at[b, :, columns(to)],
            dst_ref=bufs[kind].at[b, span(slot)],
            send_sem=kv_send.at[b, kind, d],
            recv_sem=kv_recv.at[b, kind, d],
            device_id={"tp": to},
            device_id_type=MESH,
        )

    def kv_own(b, kind):
        return pltpu.make_async_copy(
            hbms[kind].at[b, :, columns(me)], bufs[kind].at[b, span(me)], own_sem.at[b, kind]
        )

    def ad_copy(which, d, slot, to):
        src, dst = ((down_hbm, dbuf), (up_hbm, ubuf))[which]
        return pltpu.make_async_remote_copy(
            src_ref=src.at[to],
            dst_ref=dst.at[slot],
            send_sem=ad_send.at[which, d],
            recv_sem=ad_recv.at[which, d],
            device_id={"rep": to},
            device_id_type=MESH,
        )

    def ad_self(which):
        src, dst = ((down_hbm, dbuf), (up_hbm, ubuf))[which]
        return pltpu.make_async_copy(src.at[my_rep], dst.at[my_rep], ad_own.at[which])

    def row_copy(b, d, slot, to):
        return pltpu.make_async_remote_copy(
            src_ref=rows_all.at[slot, b],
            dst_ref=rows_all.at[slot, b],
            send_sem=row_send.at[b, d],
            recv_sem=row_recv.at[b, d],
            device_id={"tp": to},
            device_id_type=MESH,
        )

    def low_copy(b, d, slot, to):
        return pltpu.make_async_remote_copy(
            src_ref=low_all.at[slot, b],
            dst_ref=low_all.at[slot, b],
            send_sem=low_send.at[b, d],
            recv_sem=low_recv.at[b, d],
            device_id={"tp": to},
            device_id_type=MESH,
        )

    for b in range(blocks):
        for kind in range(2):
            for d in range(1, n):
                kv_copy(b, kind, d, me, peer(d)).start()
            kv_own(b, kind).start()
    for which in range(2):
        for d in range(1, reps):
            ad_copy(which, d, my_rep, rpeer(d)).start()
        ad_self(which).start()
    w_copy = pltpu.make_async_copy(w_hbm, wbuf, w_sem)
    w_copy.start()

    def kv_wait(b, kind):
        kv_own(b, kind).wait()
        for d in range(1, n):
            kv_copy(b, kind, d, source(d), peer(d)).wait_recv()

    scale = 1.0 / math.sqrt(hd)
    group = 2 if heads % 2 == 0 else 1
    total = n * padded

    def weigh(b):
        row = lax.rem(
            lax.broadcasted_iota(jnp.int32, (group * block_rows, 1), 0), jnp.int32(block_rows)
        )
        col = lax.broadcasted_iota(jnp.int32, (1, total), 1)
        if padded != chunk:
            part = col // padded
            inner = col - part * padded
            col = jnp.where(inner < chunk, part * chunk + inner, jnp.int32(1 << 30))
        limit = row + off_ref[b]

        @pl.loop(0, heads // group)
        def _(g):
            pieces = [
                q_ref[
                    pl.ds(b * block_rows, block_rows),
                    pl.ds(pl.multiple_of((g * group + j) * hd, hd), hd),
                ]
                for j in range(group)
            ]
            q = jnp.concatenate(pieces, axis=0)
            s = lax.dot_general(
                q, kbuf[b], (((1,), (1,)), ((), ())), preferred_element_type=jnp.float32
            )
            s = jnp.where(col <= limit, s * scale, -1e30)
            e = jnp.exp(s - jnp.max(s, axis=1, keepdims=True))
            inv = 1.0 / jnp.sum(e, axis=1, keepdims=True)
            probs[g] = (e * inv).astype(jnp.bfloat16)

    def gather_values(b):
        row = lax.broadcasted_iota(jnp.int32, (block_rows, 1), 0)
        live = row < len_ref[b]

        @pl.loop(0, heads // group)
        def _(g):
            o = jnp.dot(probs[g], vbuf[b], preferred_element_type=jnp.float32)
            for j in range(group):
                piece = jnp.where(live, o[j * block_rows : (j + 1) * block_rows], 0.0)
                rows_all[
                    me, b, :, pl.ds(pl.multiple_of((g * group + j) * hd, hd), hd)
                ] = piece.astype(jnp.bfloat16)

    rank_part = dbuf.shape[2]

    def lower(b):
        for r in range(reps):
            low_all[me, b, r * rank_part : (r + 1) * rank_part, :] = lax.dot_general(
                dbuf[r, b],
                rows_all[me, b],
                (((1,), (1,)), ((), ())),
                preferred_element_type=jnp.float32,
            )

    for b in range(blocks):
        kv_wait(b, 0)
        weigh(b)
        kv_wait(b, 1)
        gather_values(b)
        for d in range(1, n):
            row_copy(b, d, me, peer(d)).start()
        if b == 0:
            for which in range(2):
                ad_self(which).wait()
                for d in range(1, reps):
                    ad_copy(which, d, rsource(d), rpeer(d)).wait_recv()
        lower(b)
        for d in range(1, n):
            low_copy(b, d, me, peer(d)).start()

    w_copy.wait()
    for b in range(blocks):

        def project(t):
            return jnp.dot(
                rows_all[t, b],
                wbuf[pl.ds(pl.multiple_of(t * width, width), width), :],
                preferred_element_type=jnp.float32,
            )

        acc = project(me)
        low = low_all[me, b]
        for d in range(1, n):
            row_copy(b, d, source(d), peer(d)).wait_recv()
            acc += project(source(d))
        for d in range(1, n):
            low_copy(b, d, source(d), peer(d)).wait_recv()
            low += low_all[source(d), b]
        low = low.astype(jnp.bfloat16)
        for r in range(reps):
            acc += lax.dot_general(
                low[r * rank_part : (r + 1) * rank_part],
                ubuf[r, b],
                (((0,), (0,)), ((), ())),
                preferred_element_type=jnp.float32,
            )
        o_ref[b * block_rows : (b + 1) * block_rows, :] = acc.astype(o_ref.dtype)

    for b in range(blocks):
        for d in range(1, n):
            for kind in range(2):
                kv_copy(b, kind, d, me, peer(d)).wait_send()
            row_copy(b, d, me, peer(d)).wait_send()
            low_copy(b, d, me, peer(d)).wait_send()
    for which in range(2):
        for d in range(1, reps):
            ad_copy(which, d, my_rep, rpeer(d)).wait_send()


def on_device(
    queries,
    keys,
    values,
    lengths,
    offsets,
    tenants,
    tenant_storage_rows,
    output_weight,
    adapter_down_factors,
    adapter_up_factors,
):
    n = lax.axis_size("tp")
    reps = lax.axis_size("rep")
    blocks, chunk, kv_heads, hd = keys.shape
    row_count, width = queries.shape
    block_rows = row_count // blocks
    copies = n // kv_heads
    out_width = output_weight.shape[1]
    rank_part = adapter_down_factors.shape[1]
    kept = kv_heads * hd

    all_tenants = lax.all_gather(tenants, "rep", axis=0, tiled=True)
    catalog = jnp.arange(tenant_storage_rows.shape[0], dtype=jnp.int32)
    slots = jnp.sum(
        jnp.where(all_tenants[:, None] == catalog[None, :], tenant_storage_rows[None, :], 0), axis=1
    )
    selected_down = jnp.take(adapter_down_factors, slots, axis=0).reshape(
        reps, blocks, rank_part, adapter_down_factors.shape[2]
    )
    selected_up = jnp.take(adapter_up_factors, slots, axis=0).reshape(
        reps, blocks, rank_part, adapter_up_factors.shape[2]
    )

    flat_keys = keys.reshape(blocks, chunk, kept)
    flat_values = values.reshape(blocks, chunk, kept)
    padded = -(-chunk // 16) * 16
    if padded != chunk:
        extra = ((0, 0), (0, padded - chunk), (0, 0))
        flat_keys = jnp.pad(flat_keys, extra)
        flat_values = jnp.pad(flat_values, extra)

    heads = width // hd
    group = 2 if heads % 2 == 0 else 1
    bf16, f32 = jnp.bfloat16, jnp.float32
    dma = pltpu.SemaphoreType.DMA
    anywhere = pl.BlockSpec(memory_space=pl.ANY)
    smem = pl.BlockSpec(memory_space=pltpu.SMEM)
    vmem = pl.BlockSpec(memory_space=pltpu.VMEM)
    return pl.pallas_call(
        functools.partial(kernel, n, reps, copies, chunk, kept),
        out_shape=jax.ShapeDtypeStruct((row_count, out_width), bf16),
        in_specs=[smem, smem, vmem] + [anywhere] * 5,
        out_specs=vmem,
        scratch_shapes=[
            pltpu.VMEM((blocks, n * padded, hd), bf16),
            pltpu.VMEM((blocks, n * padded, hd), bf16),
            pltpu.VMEM((heads // group, group * block_rows, n * padded), bf16),
            pltpu.VMEM((n, blocks, block_rows, width), bf16),
            pltpu.VMEM((n, blocks, reps * rank_part, block_rows), f32),
            pltpu.VMEM((reps, blocks, rank_part, width), bf16),
            pltpu.VMEM((reps, blocks, rank_part, out_width), bf16),
            pltpu.VMEM((n * width, out_width), bf16),
            dma((blocks, 2, n)),
            dma((blocks, 2, n)),
            dma((blocks, 2)),
            dma,
            dma((2, reps)),
            dma((2, reps)),
            dma((2,)),
            dma((blocks, n)),
            dma((blocks, n)),
            dma((blocks, n)),
            dma((blocks, n)),
        ],
        compiler_params=pltpu.CompilerParams(
            collective_id=0, has_side_effects=True, vmem_limit_bytes=52 * 1024 * 1024
        ),
        cost_estimate=pl.CostEstimate(
            flops=4 * row_count * width * n * chunk + 2 * row_count * n * width * out_width,
            bytes_accessed=2 * n * width * out_width + 8 * blocks * chunk * kept,
            transcendentals=row_count * heads * n * chunk,
        ),
    )(
        offsets,
        lengths,
        queries,
        flat_keys,
        flat_values,
        output_weight,
        selected_down,
        selected_up,
    )


def solution(mesh):
    return jax.shard_map(
        on_device,
        mesh=mesh,
        in_specs=(
            P(("groups", "rep"), "tp"),
            P(("groups", "rep"), "tp", None, None),
            P(("groups", "rep"), "tp", None, None),
            P(("groups", "rep")),
            P(("groups", "rep")),
            P(("groups", "rep")),
            P(),
            P(None, "tp"),
            P(None, "rep", "tp"),
            P(None, "rep", "tp"),
        ),
        out_specs=P(("groups", "rep"), "tp"),
        check_vma=False,
    )
```

time: 191 us -> 150 us (0.79)
  Pallas kernels: 0 us -> 128 us
  waiting for transfers between devices: 94.3 us -> 0 us
  matrix products: 35.7 us -> 0 us
  starting transfers between devices: 13.5 us -> 0 us
  between operations: 14.2 us -> 0.73 us
  blocking collectives: 14 us -> 6.35 us
    pallas_call x0 -> x1, Pallas kernels: none -> 128 us  [on_device(): pl.pallas_call(functools.partial(kernel, n, reps, copies, chunk, kept), o...]
    all_to_all x3 -> x0, waiting for transfers between devices: 59 us -> none  [the longest x1 34.5 us: on_device(): lax.all_to_all(sent_keys, 'tp', split_axis=2, concat_axis=1, tiled=True)]
    all_gather x2 -> x0, waiting for transfers between devices: 35.2 us -> none  [the longest x1 20.6 us: on_device(): piece_down = lax.all_gather(down_factor_rows, 'tp', axis=2, tiled=True)]
    dot_general x3 -> x0, matrix products: 20.9 us -> none  [the longest x1 9.92 us: attend(): jnp.einsum('lzug,lgy->luzy', probabilities, head_values, preferred_elemen...]
    sub x1 -> x0, matrix products: 14.8 us -> none  [attend(): weights = jnp.exp(scores - top_score)]
    all_to_all x3 -> x0, starting transfers between devices: 13.4 us -> none  [the longest x1 6.45 us: on_device(): lax.all_to_all(sent_keys, 'tp', split_axis=2, concat_axis=1, tiled=True)]
    all_to_all x1 -> x0, blocking collectives: 9.11 us -> none  [on_device(): lax.all_to_all(selected_up, 'rep', split_axis=0, concat_axis=2, tiled=True)]
    reshape x0 -> x2, local copies, waits for them, and re-layouts: none -> 5.4 us  [the longest x1 3.88 us: on_device(): flat_keys = keys.reshape(blocks, chunk, kept)]
  transfers between devices with their start and end apart: 5 -> 0, of which waited for: 5 -> 0; matrix products, arithmetic and copies ran while one was open for 20% -> 0% of each run, Pallas kernels for 0% -> 0%
where the time goes in v1:
time: 150 us
  Pallas kernels  128 us (85%)
  local copies, waits for them, and re-layouts  14.4 us (10%)
  blocking collectives  6.35 us (4%)
    pallas_call x1, Pallas kernels, on_device(): pl.pallas_call(functools.partial(kernel, n, reps, copies, chunk, kept), o...  128 us
    unnamed x1, blocking collectives  6.35 us
    reshape x1, local copies, waits for them, and re-layouts, on_device(): flat_keys = keys.reshape(blocks, chunk, kept)  3.88 us
    gather x1, local copies, waits for them, and re-layouts, on_device(): jnp.take(adapter_up_factors, slots, axis=0)  3.11 us
    unnamed x12, local copies, waits for them, and re-layouts  3.08 us

profile of v1, /device:TPU:0, one launch (start us, length us, event | category | flops | bytes accessed | tf_op | source)
XLA Modules:
  0.0 150.2 jit_solution(13971929799904478308)
XLA Ops:
  0.0 0.0 copy-start.3
  0.0 1.4 dynamic-slice
  2.0 0.9 dynamic-update-slice
  2.9 6.3 %all-reduce = s32[8]{0:T(128)S(1)} all-reduce(s32[8]{0:T(128)S(1)} %dynamic-update-slice), channel_id=1, replica_groups=mesh['groups'=2,'rep'=4,'tp'=4] {'rep'}, use_global_device_ids=true, to_apply=%add | all-reduce | flops 8 | bytes 64
  9.2 0.8 select_reduce_fusion
  10.1 0.1 reduce_sum.14
  10.2 2.8 %gather_fusion = bf16[8,16,1024]{2,1,0:T(8,128)(2,1)S(1)} fusion(bf16[128,16,1024]{2,1,0:T(8,128)(2,1)} %param.18, s32[1024]{0:T(1024)S(1)} %pad_clamp_fusion), kind=kCustom, calls=%fused_computation | custom fusion | bytes 524320 | tf_op jit(solution)/shard_map/jit(_take)/gather | solution.py:292
  12.9 0.0 copy-start
  13.0 0.0 copy-start.1
  13.0 0.0 copy-start.2
  13.0 0.1 broadcast_select_fusion.1.down_hbm
  13.1 3.1 %gather_fusion.1 = bf16[8,16,1280]{2,1,0:T(8,128)(2,1)S(1)} fusion(bf16[128,16,1280]{2,1,0:T(8,128)(2,1)} %param.19, s32[1024]{0:T(1024)S(1)} %pad_clamp_fusion), kind=kCustom, calls=%fused_computation.1 | custom fusion | bytes 655392 | tf_op jit(solution)/shard_map/jit(_take)/gather | solution.py:295
  16.2 0.1 broadcast_select_fusion.up_hbm
  16.3 3.9 %reshape.33.k_hbm = bf16[2,800,512]{2,1,0:T(8,128)(2,1)} reshape(bf16[2,800,4,128]{3,2,1,0:T(4,128)(2,1)} %param.11) | data formatting | bytes 3276800 | tf_op jit(solution)/shard_map/reshape | solution.py:299
  20.2 0.0 copy-done.3
  20.2 1.5 %reshape.34.v_hbm = bf16[2,800,512]{2,1,0:T(8,128)(2,1)} reshape(bf16[2,800,4,128]{3,2,1,0:T(4,128)(2,1)S(1)} %copy-done.3) | data formatting | bytes 3276800 | tf_op jit(solution)/shard_map/reshape | solution.py:300
  21.7 0.0 copy-done
  21.7 0.0 copy-done.1
  21.7 0.0 copy-done.2
  21.7 127.6 %shard_map.100 = bf16[256,1280]{1,0:T(8,128)(2,1)S(1)} custom-call(s32[2]{0:T(128)S(1)} %copy-done.1, s32[2]{0:T(128)S(1)} %copy-done.2, bf16[256,1024]{1,0:T(8,128)(2,1)S(1)} %copy-done, bf16[2,800,512]{2,1,0:T(8,128)(2,1)} %reshape.33.k_hbm, bf16[2,800,512]{2,1,0:T(8,128)(2,1)} %reshape.34.v_hbm, bf16[4096,1280]{1,0:T(8,128)(2,1)} %w_hbm.1, ...), custom_call_target="tpu_custom_call" | custom-call | flops 6039797760 | bytes 17039360 | tf_op jit(solution)/shard_map/pallas_call | solution.py:314
  149.3 0.8 copy.13
  (4 shorter events, 0.0 us)
Async XLA Ops:
  0.0 20.2 %copy-start.3 = (bf16[2,800,4,128]{3,2,1,0:T(4,128)(2,1)S(1)}, bf16[2,800,4,128]{3,2,1,0:T(4,128)(2,1)}, u32[]{:S(2)}) copy-start(bf16[2,800,4,128]{3,2,1,0:T(4,128)(2,1)} %param.12) | copy-start | bytes 4915204
  12.9 8.8 %copy-start = (bf16[256,1024]{1,0:T(8,128)(2,1)S(1)}, bf16[256,1024]{1,0:T(8,128)(2,1)}, u32[]{:S(2)}) copy-start(bf16[256,1024]{1,0:T(8,128)(2,1)} %q_ref.1) | copy-start | bytes 1572868
  13.0 8.8 %copy-start.1 = (s32[2]{0:T(128)S(1)}, s32[2]{0:T(128)}, u32[]{:S(2)}) copy-start(s32[2]{0:T(128)} %off_ref.1) | copy-start | bytes 28
  13.0 8.7 %copy-start.2 = (s32[2]{0:T(128)S(1)}, s32[2]{0:T(128)}, u32[]{:S(2)}) copy-start(s32[2]{0:T(128)} %len_ref.1) | copy-start | bytes 28

commit v2 on v1

--- a/solution.py
+++ b/solution.py
@@ -19,6 +19,8 @@
     kept,
     off_ref,
     len_ref,
+    storage_ref,
+    tenant_ref,
     q_ref,
     k_hbm,
     v_hbm,
@@ -31,6 +33,13 @@
     probs,
     rows_all,
     low_all,
+    acc,
+    tenants_got,
+    tenants_smem,
+    down_table,
+    up_table,
+    down_sel,
+    up_sel,
     dbuf,
     ubuf,
     wbuf,
@@ -41,6 +50,10 @@
     ad_send,
     ad_recv,
     ad_own,
+    ten_send,
+    ten_recv,
+    ten_sem,
+    table_sem,
     row_send,
     row_recv,
     low_send,
@@ -99,7 +112,7 @@
         )
 
     def ad_copy(which, d, slot, to):
-        src, dst = ((down_hbm, dbuf), (up_hbm, ubuf))[which]
+        src, dst = ((down_sel, dbuf), (up_sel, ubuf))[which]
         return pltpu.make_async_remote_copy(
             src_ref=src.at[to],
             dst_ref=dst.at[slot],
@@ -110,16 +123,68 @@
         )
 
     def ad_self(which):
-        src, dst = ((down_hbm, dbuf), (up_hbm, ubuf))[which]
+        src, dst = ((down_sel, dbuf), (up_sel, ubuf))[which]
         return pltpu.make_async_copy(src.at[my_rep], dst.at[my_rep], ad_own.at[which])
 
-    def row_copy(b, d, slot, to):
+    def row_copy(b, way, t, slot, to):
         return pltpu.make_async_remote_copy(
             src_ref=rows_all.at[slot, b],
             dst_ref=rows_all.at[slot, b],
-            send_sem=row_send.at[b, d],
-            recv_sem=row_recv.at[b, d],
+            send_sem=row_send.at[b, way, t],
+            recv_sem=row_recv.at[b, way, t],
             device_id={"tp": to},
+            device_id_type=MESH,
+        )
+
+    def sends(t):
+        return ((me >= t) & (me < n - 1), (me + t <= n - 1) & (me > 0))
+
+    def gets(t):
+        return (me >= t + 1, me + t + 1 <= n - 1)
+
+    def send_rows(b, t):
+        up_too, down_too = sends(t)
+
+        @pl.when(up_too)
+        def _():
+            row_copy(b, 0, t, me - t, me + 1).start()
+
+        @pl.when(down_too)
+        def _():
+            row_copy(b, 1, t, me + t, me - 1).start()
+
+    def sent_rows(b, t):
+        up_too, down_too = sends(t)
+
+        @pl.when(up_too)
+        def _():
+            row_copy(b, 0, t, me - t, me + 1).wait_send()
+
+        @pl.when(down_too)
+        def _():
+            row_copy(b, 1, t, me + t, me - 1).wait_send()
+
+    def take_rows(b, t):
+        below, above = gets(t)
+
+        @pl.when(below)
+        def _():
+            row_copy(b, 0, t, me - 1 - t, me - 1).wait_recv()
+
+        @pl.when(above)
+        def _():
+            row_copy(b, 1, t, me + 1 + t, me + 1).wait_recv()
+
+        if t + 1 <= n - 2:
+            send_rows(b, t + 1)
+
+    def tenant_copy(d, slot, to):
+        return pltpu.make_async_remote_copy(
+            src_ref=tenant_ref,
+            dst_ref=tenants_got.at[slot],
+            send_sem=ten_send.at[d],
+            recv_sem=ten_recv.at[d],
+            device_id={"rep": to},
             device_id_type=MESH,
         )
 
@@ -133,17 +198,41 @@
             device_id_type=MESH,
         )
 
+    for d in range(1, reps):
+        tenant_copy(d, my_rep, rpeer(d)).start()
+    tenant_own = pltpu.make_async_copy(tenant_ref, tenants_got.at[my_rep], ten_sem.at[0])
+    tenant_own.start()
     for b in range(blocks):
         for kind in range(2):
             for d in range(1, n):
                 kv_copy(b, kind, d, me, peer(d)).start()
             kv_own(b, kind).start()
+    tables = [
+        pltpu.make_async_copy(down_hbm, down_table, table_sem.at[0]),
+        pltpu.make_async_copy(up_hbm, up_table, table_sem.at[1]),
+    ]
+    for copy in tables:
+        copy.start()
+    w_copy = pltpu.make_async_copy(w_hbm, wbuf, w_sem)
+    w_copy.start()
+
+    tenant_own.wait()
+    for d in range(1, reps):
+        tenant_copy(d, rsource(d), rpeer(d)).wait_recv()
+    to_smem = pltpu.make_async_copy(tenants_got, tenants_smem, ten_sem.at[1])
+    to_smem.start()
+    to_smem.wait()
+    for copy in tables:
+        copy.wait()
+    for r in range(reps):
+        for b in range(blocks):
+            slot = storage_ref[tenants_smem[r, 0, b]]
+            down_sel[r, b] = down_table[slot]
+            up_sel[r, b] = up_table[slot]
     for which in range(2):
         for d in range(1, reps):
             ad_copy(which, d, my_rep, rpeer(d)).start()
         ad_self(which).start()
-    w_copy = pltpu.make_async_copy(w_hbm, wbuf, w_sem)
-    w_copy.start()
 
     def kv_wait(b, kind):
         kv_own(b, kind).wait()
@@ -210,10 +299,11 @@
     for b in range(blocks):
         kv_wait(b, 0)
         weigh(b)
+        if b > 0 and n > 1:
+            take_rows(b - 1, 0)
         kv_wait(b, 1)
         gather_values(b)
-        for d in range(1, n):
-            row_copy(b, d, me, peer(d)).start()
+        send_rows(b, 0)
         if b == 0:
             for which in range(2):
                 ad_self(which).wait()
@@ -223,40 +313,55 @@
         for d in range(1, n):
             low_copy(b, d, me, peer(d)).start()
 
+    def project(b, t):
+        return jnp.dot(
+            rows_all[t, b],
+            wbuf[pl.ds(pl.multiple_of(t * width, width), width), :],
+            preferred_element_type=jnp.float32,
+        )
+
     w_copy.wait()
     for b in range(blocks):
-
-        def project(t):
-            return jnp.dot(
-                rows_all[t, b],
-                wbuf[pl.ds(pl.multiple_of(t * width, width), width), :],
-                preferred_element_type=jnp.float32,
-            )
-
-        acc = project(me)
+        acc[b] = project(b, me)
+    for t in range(n - 1):
+        for b in range(blocks):
+            if t > 0 or b == blocks - 1:
+                take_rows(b, t)
+            below, above = gets(t)
+
+            @pl.when(below)
+            def _():
+                acc[b] += project(b, me - 1 - t)
+
+            @pl.when(above)
+            def _():
+                acc[b] += project(b, me + 1 + t)
+
+    for b in range(blocks):
         low = low_all[me, b]
-        for d in range(1, n):
-            row_copy(b, d, source(d), peer(d)).wait_recv()
-            acc += project(source(d))
         for d in range(1, n):
             low_copy(b, d, source(d), peer(d)).wait_recv()
             low += low_all[source(d), b]
         low = low.astype(jnp.bfloat16)
+        mixed = acc[b]
         for r in range(reps):
-            acc += lax.dot_general(
+            mixed += lax.dot_general(
                 low[r * rank_part : (r + 1) * rank_part],
                 ubuf[r, b],
                 (((0,), (0,)), ((), ())),
                 preferred_element_type=jnp.float32,
             )
-        o_ref[b * block_rows : (b + 1) * block_rows, :] = acc.astype(o_ref.dtype)
+        o_ref[b * block_rows : (b + 1) * block_rows, :] = mixed.astype(o_ref.dtype)
 
     for b in range(blocks):
         for d in range(1, n):
             for kind in range(2):
                 kv_copy(b, kind, d, me, peer(d)).wait_send()
-            row_copy(b, d, me, peer(d)).wait_send()
             low_copy(b, d, me, peer(d)).wait_send()
+        for t in range(n - 1):
+            sent_rows(b, t)
+    for d in range(1, reps):
+        tenant_copy(d, my_rep, rpeer(d)).wait_send()
     for which in range(2):
         for d in range(1, reps):
             ad_copy(which, d, my_rep, rpeer(d)).wait_send()
@@ -284,17 +389,8 @@
     rank_part = adapter_down_factors.shape[1]
     kept = kv_heads * hd
 
-    all_tenants = lax.all_gather(tenants, "rep", axis=0, tiled=True)
-    catalog = jnp.arange(tenant_storage_rows.shape[0], dtype=jnp.int32)
-    slots = jnp.sum(
-        jnp.where(all_tenants[:, None] == catalog[None, :], tenant_storage_rows[None, :], 0), axis=1
-    )
-    selected_down = jnp.take(adapter_down_factors, slots, axis=0).reshape(
-        reps, blocks, rank_part, adapter_down_factors.shape[2]
-    )
-    selected_up = jnp.take(adapter_up_factors, slots, axis=0).reshape(
-        reps, blocks, rank_part, adapter_up_factors.shape[2]
-    )
+    stored = adapter_down_factors.shape[0]
+    tenant_tile = jnp.pad(tenants[None, :], ((0, 7), (0, 128 - blocks)))
 
     flat_keys = keys.reshape(blocks, chunk, kept)
     flat_values = values.reshape(blocks, chunk, kept)
@@ -314,7 +410,7 @@
     return pl.pallas_call(
         functools.partial(kernel, n, reps, copies, chunk, kept),
         out_shape=jax.ShapeDtypeStruct((row_count, out_width), bf16),
-        in_specs=[smem, smem, vmem] + [anywhere] * 5,
+        in_specs=[smem, smem, smem, vmem, vmem] + [anywhere] * 5,
         out_specs=vmem,
         scratch_shapes=[
             pltpu.VMEM((blocks, n * padded, hd), bf16),
@@ -322,6 +418,13 @@
             pltpu.VMEM((heads // group, group * block_rows, n * padded), bf16),
             pltpu.VMEM((n, blocks, block_rows, width), bf16),
             pltpu.VMEM((n, blocks, reps * rank_part, block_rows), f32),
+            pltpu.VMEM((blocks, block_rows, out_width), f32),
+            pltpu.VMEM((reps, 8, 128), jnp.int32),
+            pltpu.SMEM((reps, 8, 128), jnp.int32),
+            pltpu.VMEM((stored, rank_part, width), bf16),
+            pltpu.VMEM((stored, rank_part, out_width), bf16),
+            pltpu.VMEM((reps, blocks, rank_part, width), bf16),
+            pltpu.VMEM((reps, blocks, rank_part, out_width), bf16),
             pltpu.VMEM((reps, blocks, rank_part, width), bf16),
             pltpu.VMEM((reps, blocks, rank_part, out_width), bf16),
             pltpu.VMEM((n * width, out_width), bf16),
@@ -332,8 +435,12 @@
             dma((2, reps)),
             dma((2, reps)),
             dma((2,)),
-            dma((blocks, n)),
-            dma((blocks, n)),
+            dma((reps,)),
+            dma((reps,)),
+            dma((2,)),
+            dma((2,)),
+            dma((blocks, 2, n)),
+            dma((blocks, 2, n)),
             dma((blocks, n)),
             dma((blocks, n)),
         ],
@@ -348,12 +455,14 @@
     )(
         offsets,
         lengths,
+        tenant_storage_rows,
+        tenant_tile,
         queries,
         flat_keys,
         flat_values,
         output_weight,
-        selected_down,
-        selected_up,
+        adapter_down_factors,
+        adapter_up_factors,
     )
 
 

time: 150 us -> 126 us (0.84)
  Pallas kernels: 128 us -> 119 us
  local copies, waits for them, and re-layouts: 14.4 us -> 7.07 us
  blocking collectives: 6.35 us -> 0 us
    pallas_call x1, Pallas kernels: 128 us -> 119 us  [on_device(): pl.pallas_call(functools.partial(kernel, n, reps, copies, chunk, kept), o...]
    unnamed x1 -> x0, blocking collectives: 6.35 us -> none
    gather x2 -> x0, local copies, waits for them, and re-layouts: 5.86 us -> none  [the longest x1 3.11 us: on_device(): jnp.take(adapter_up_factors, slots, axis=0)]
    unnamed x12 -> x11, local copies, waits for them, and re-layouts: 3.08 us -> 0.86 us
where the time goes in v2:
time: 126 us
  Pallas kernels  119 us (94%)
  local copies, waits for them, and re-layouts  7.07 us (6%)
    pallas_call x1, Pallas kernels, on_device(): pl.pallas_call(functools.partial(kernel, n, reps, copies, chunk, kept), o...  119 us
    reshape x1, local copies, waits for them, and re-layouts, on_device(): flat_keys = keys.reshape(blocks, chunk, kept)  3.99 us

profile of v2, /device:TPU:0, one launch (start us, length us, event | category | flops | bytes accessed | tf_op | source)
XLA Modules:
  0.0 126.3 jit_solution(1533276863226635469)
XLA Ops:
  0.0 0.7 pad.4.tenant_ref
  0.7 0.0 copy-start.4
  0.7 4.0 %reshape.6.k_hbm = bf16[2,800,512]{2,1,0:T(8,128)(2,1)} reshape(bf16[2,800,4,128]{3,2,1,0:T(4,128)(2,1)} %param.11) | data formatting | bytes 3276800 | tf_op jit(solution)/shard_map/reshape | solution.py:395
  4.7 0.0 copy-done.4
  4.7 0.0 copy-start
  4.7 0.0 copy-start.1
  4.7 0.0 copy-start.2
  4.7 0.0 copy-start.3
  4.7 1.6 %reshape.7.v_hbm = bf16[2,800,512]{2,1,0:T(8,128)(2,1)} reshape(bf16[2,800,4,128]{3,2,1,0:T(4,128)(2,1)S(1)} %copy-done.4) | data formatting | bytes 3276800 | tf_op jit(solution)/shard_map/reshape | solution.py:396
  6.2 0.0 copy-done
  6.2 0.0 copy-done.1
  6.2 0.0 copy-done.2
  6.3 0.0 copy-done.3
  6.3 119.2 %shard_map.100 = bf16[256,1280]{1,0:T(8,128)(2,1)S(1)} custom-call(s32[2]{0:T(128)S(1)} %copy-done.1, s32[2]{0:T(128)S(1)} %copy-done.2, s32[128]{0:T(128)S(1)} %copy-done.3, s32[8,128]{1,0:T(8,128)S(1)} %pad.4.tenant_ref, bf16[256,1024]{1,0:T(8,128)(2,1)S(1)} %copy-done, bf16[2,800,512]{2,1,0:T(8,128)(2,1)} %reshape.6.k_hbm, ...), custom_call_target="tpu_custom_call" | custom-call | flops 6039797760 | bytes 17039360 | tf_op jit(solution)/shard_map/pallas_call | solution.py:410
  125.5 0.8 copy.12
Async XLA Ops:
  0.7 4.0 %copy-start.4 = (bf16[2,800,4,128]{3,2,1,0:T(4,128)(2,1)S(1)}, bf16[2,800,4,128]{3,2,1,0:T(4,128)(2,1)}, u32[]{:S(2)}) copy-start(bf16[2,800,4,128]{3,2,1,0:T(4,128)(2,1)} %param.12) | copy-start | bytes 4915204
  4.7 1.6 %copy-start = (bf16[256,1024]{1,0:T(8,128)(2,1)S(1)}, bf16[256,1024]{1,0:T(8,128)(2,1)}, u32[]{:S(2)}) copy-start(bf16[256,1024]{1,0:T(8,128)(2,1)} %q_ref.1) | copy-start | bytes 1572868
  4.7 1.6 %copy-start.1 = (s32[2]{0:T(128)S(1)}, s32[2]{0:T(128)}, u32[]{:S(2)}) copy-start(s32[2]{0:T(128)} %off_ref.1) | copy-start | bytes 28
  4.7 1.6 %copy-start.2 = (s32[2]{0:T(128)S(1)}, s32[2]{0:T(128)}, u32[]{:S(2)}) copy-start(s32[2]{0:T(128)} %len_ref.1) | copy-start | bytes 28
  4.7 1.6 %copy-start.3 = (s32[128]{0:T(128)S(1)}, s32[128]{0:T(128)}, u32[]{:S(2)}) copy-start(s32[128]{0:T(128)} %storage_ref.1) | copy-start | bytes 1540

commit v3 on v2

--- a/solution.py
+++ b/solution.py
@@ -65,6 +65,7 @@
     block_rows = q_ref.shape[0] // blocks
     width = q_ref.shape[1]
     heads = width // hd
+    parts = rows_all.shape[2]
     me = lax.axis_index("tp")
     my_rep = lax.axis_index("rep")
 
@@ -126,12 +127,12 @@
         src, dst = ((down_sel, dbuf), (up_sel, ubuf))[which]
         return pltpu.make_async_copy(src.at[my_rep], dst.at[my_rep], ad_own.at[which])
 
-    def row_copy(b, way, t, slot, to):
+    def row_copy(b, way, t, part, slot, to):
         return pltpu.make_async_remote_copy(
-            src_ref=rows_all.at[slot, b],
-            dst_ref=rows_all.at[slot, b],
-            send_sem=row_send.at[b, way, t],
-            recv_sem=row_recv.at[b, way, t],
+            src_ref=rows_all.at[slot, b, part],
+            dst_ref=rows_all.at[slot, b, part],
+            send_sem=row_send.at[b, way, t * parts + part],
+            recv_sem=row_recv.at[b, way, t * parts + part],
             device_id={"tp": to},
             device_id_type=MESH,
         )
@@ -142,41 +143,42 @@
     def gets(t):
         return (me >= t + 1, me + t + 1 <= n - 1)
 
-    def send_rows(b, t):
+    def send_rows(b, t, part):
         up_too, down_too = sends(t)
 
         @pl.when(up_too)
         def _():
-            row_copy(b, 0, t, me - t, me + 1).start()
+            row_copy(b, 0, t, part, me - t, me + 1).start()
 
         @pl.when(down_too)
         def _():
-            row_copy(b, 1, t, me + t, me - 1).start()
-
-    def sent_rows(b, t):
+            row_copy(b, 1, t, part, me + t, me - 1).start()
+
+    def sent_rows(b, t, part):
         up_too, down_too = sends(t)
 
         @pl.when(up_too)
         def _():
-            row_copy(b, 0, t, me - t, me + 1).wait_send()
+            row_copy(b, 0, t, part, me - t, me + 1).wait_send()
 
         @pl.when(down_too)
         def _():
-            row_copy(b, 1, t, me + t, me - 1).wait_send()
+            row_copy(b, 1, t, part, me + t, me - 1).wait_send()
 
     def take_rows(b, t):
         below, above = gets(t)
-
-        @pl.when(below)
-        def _():
-            row_copy(b, 0, t, me - 1 - t, me - 1).wait_recv()
-
-        @pl.when(above)
-        def _():
-            row_copy(b, 1, t, me + 1 + t, me + 1).wait_recv()
-
-        if t + 1 <= n - 2:
-            send_rows(b, t + 1)
+        for part in range(parts):
+
+            @pl.when(below)
+            def _():
+                row_copy(b, 0, t, part, me - 1 - t, me - 1).wait_recv()
+
+            @pl.when(above)
+            def _():
+                row_copy(b, 1, t, part, me + 1 + t, me + 1).wait_recv()
+
+            if t + 1 <= n - 2:
+                send_rows(b, t + 1, part)
 
     def tenant_copy(d, slot, to):
         return pltpu.make_async_remote_copy(
@@ -202,11 +204,14 @@
         tenant_copy(d, my_rep, rpeer(d)).start()
     tenant_own = pltpu.make_async_copy(tenant_ref, tenants_got.at[my_rep], ten_sem.at[0])
     tenant_own.start()
+    def kv_start(b, kind):
+        for d in range(1, n):
+            kv_copy(b, kind, d, me, peer(d)).start()
+        kv_own(b, kind).start()
+
     for b in range(blocks):
         for kind in range(2):
-            for d in range(1, n):
-                kv_copy(b, kind, d, me, peer(d)).start()
-            kv_own(b, kind).start()
+            kv_start(b, kind)
     tables = [
         pltpu.make_async_copy(down_hbm, down_table, table_sem.at[0]),
         pltpu.make_async_copy(up_hbm, up_table, table_sem.at[1]),
@@ -272,28 +277,33 @@
             inv = 1.0 / jnp.sum(e, axis=1, keepdims=True)
             probs[g] = (e * inv).astype(jnp.bfloat16)
 
-    def gather_values(b):
+    def gather_values(b, part):
         row = lax.broadcasted_iota(jnp.int32, (block_rows, 1), 0)
         live = row < len_ref[b]
-
-        @pl.loop(0, heads // group)
+        steps = heads // group // parts
+
+        @pl.loop(0, steps)
         def _(g):
-            o = jnp.dot(probs[g], vbuf[b], preferred_element_type=jnp.float32)
+            o = jnp.dot(probs[part * steps + g], vbuf[b], preferred_element_type=jnp.float32)
             for j in range(group):
                 piece = jnp.where(live, o[j * block_rows : (j + 1) * block_rows], 0.0)
                 rows_all[
-                    me, b, :, pl.ds(pl.multiple_of((g * group + j) * hd, hd), hd)
+                    me, b, part, :, pl.ds(pl.multiple_of((g * group + j) * hd, hd), hd)
                 ] = piece.astype(jnp.bfloat16)
 
     rank_part = dbuf.shape[2]
+    share = width // parts
 
     def lower(b):
         for r in range(reps):
-            low_all[me, b, r * rank_part : (r + 1) * rank_part, :] = lax.dot_general(
-                dbuf[r, b],
-                rows_all[me, b],
-                (((1,), (1,)), ((), ())),
-                preferred_element_type=jnp.float32,
+            low_all[me, b, r * rank_part : (r + 1) * rank_part, :] = sum(
+                lax.dot_general(
+                    dbuf[r, b, :, p * share : (p + 1) * share],
+                    rows_all[me, b, p],
+                    (((1,), (1,)), ((), ())),
+                    preferred_element_type=jnp.float32,
+                )
+                for p in range(parts)
             )
 
     for b in range(blocks):
@@ -302,8 +312,9 @@
         if b > 0 and n > 1:
             take_rows(b - 1, 0)
         kv_wait(b, 1)
-        gather_values(b)
-        send_rows(b, 0)
+        for part in range(parts):
+            gather_values(b, part)
+            send_rows(b, 0, part)
         if b == 0:
             for which in range(2):
                 ad_self(which).wait()
@@ -314,10 +325,13 @@
             low_copy(b, d, me, peer(d)).start()
 
     def project(b, t):
-        return jnp.dot(
-            rows_all[t, b],
-            wbuf[pl.ds(pl.multiple_of(t * width, width), width), :],
-            preferred_element_type=jnp.float32,
+        return sum(
+            jnp.dot(
+                rows_all[t, b, p],
+                wbuf[pl.ds(pl.multiple_of(t * width + p * share, share), share), :],
+                preferred_element_type=jnp.float32,
+            )
+            for p in range(parts)
         )
 
     w_copy.wait()
@@ -359,7 +373,8 @@
                 kv_copy(b, kind, d, me, peer(d)).wait_send()
             low_copy(b, d, me, peer(d)).wait_send()
         for t in range(n - 1):
-            sent_rows(b, t)
+            for part in range(parts):
+                sent_rows(b, t, part)
     for d in range(1, reps):
         tenant_copy(d, my_rep, rpeer(d)).wait_send()
     for which in range(2):
@@ -402,6 +417,7 @@
 
     heads = width // hd
     group = 2 if heads % 2 == 0 else 1
+    parts = 2 if (heads // group) % 2 == 0 else 1
     bf16, f32 = jnp.bfloat16, jnp.float32
     dma = pltpu.SemaphoreType.DMA
     anywhere = pl.BlockSpec(memory_space=pl.ANY)
@@ -416,7 +432,7 @@
             pltpu.VMEM((blocks, n * padded, hd), bf16),
             pltpu.VMEM((blocks, n * padded, hd), bf16),
             pltpu.VMEM((heads // group, group * block_rows, n * padded), bf16),
-            pltpu.VMEM((n, blocks, block_rows, width), bf16),
+            pltpu.VMEM((n, blocks, parts, block_rows, width // parts), bf16),
             pltpu.VMEM((n, blocks, reps * rank_part, block_rows), f32),
             pltpu.VMEM((blocks, block_rows, out_width), f32),
             pltpu.VMEM((reps, 8, 128), jnp.int32),
@@ -439,8 +455,8 @@
             dma((reps,)),
             dma((2,)),
             dma((2,)),
-            dma((blocks, 2, n)),
-            dma((blocks, 2, n)),
+            dma((blocks, 2, n * parts)),
+            dma((blocks, 2, n * parts)),
             dma((blocks, n)),
             dma((blocks, n)),
         ],

time: 126 us -> 125 us (level)
  no operation moved by 1% of the time
where the time goes in v3:
time: 125 us
  Pallas kernels  118 us (94%)
  local copies, waits for them, and re-layouts  7.07 us (6%)
    pallas_call x1, Pallas kernels, on_device(): pl.pallas_call(functools.partial(kernel, n, reps, copies, chunk, kept), o...  118 us
    reshape x1, local copies, waits for them, and re-layouts, on_device(): flat_keys = keys.reshape(blocks, chunk, kept)  3.99 us

profile of v3, /device:TPU:0, one launch (start us, length us, event | category | flops | bytes accessed | tf_op | source)
XLA Modules:
  0.0 125.1 jit_solution(6490188604490968550)
XLA Ops:
  0.0 0.7 pad.4.tenant_ref
  0.7 0.0 copy-start.4
  0.7 4.0 %reshape.6.k_hbm = bf16[2,800,512]{2,1,0:T(8,128)(2,1)} reshape(bf16[2,800,4,128]{3,2,1,0:T(4,128)(2,1)} %param.11) | data formatting | bytes 3276800 | tf_op jit(solution)/shard_map/reshape | solution.py:410
  4.7 0.0 copy-done.4
  4.7 0.0 copy-start
  4.7 0.0 copy-start.1
  4.7 0.0 copy-start.2
  4.7 0.0 copy-start.3
  4.7 1.6 %reshape.7.v_hbm = bf16[2,800,512]{2,1,0:T(8,128)(2,1)} reshape(bf16[2,800,4,128]{3,2,1,0:T(4,128)(2,1)S(1)} %copy-done.4) | data formatting | bytes 3276800 | tf_op jit(solution)/shard_map/reshape | solution.py:411
  6.2 0.0 copy-done
  6.2 0.0 copy-done.1
  6.2 0.0 copy-done.2
  6.3 0.0 copy-done.3
  6.3 118.0 %shard_map.100 = bf16[256,1280]{1,0:T(8,128)(2,1)S(1)} custom-call(s32[2]{0:T(128)S(1)} %copy-done.1, s32[2]{0:T(128)S(1)} %copy-done.2, s32[128]{0:T(128)S(1)} %copy-done.3, s32[8,128]{1,0:T(8,128)S(1)} %pad.4.tenant_ref, bf16[256,1024]{1,0:T(8,128)(2,1)S(1)} %copy-done, bf16[2,800,512]{2,1,0:T(8,128)(2,1)} %reshape.6.k_hbm, ...), custom_call_target="tpu_custom_call" | custom-call | flops 6039797760 | bytes 17039360 | tf_op jit(solution)/shard_map/pallas_call | solution.py:426
  124.3 0.8 copy.12
Async XLA Ops:
  0.7 4.0 %copy-start.4 = (bf16[2,800,4,128]{3,2,1,0:T(4,128)(2,1)S(1)}, bf16[2,800,4,128]{3,2,1,0:T(4,128)(2,1)}, u32[]{:S(2)}) copy-start(bf16[2,800,4,128]{3,2,1,0:T(4,128)(2,1)} %param.12) | copy-start | bytes 4915204
  4.7 1.6 %copy-start = (bf16[256,1024]{1,0:T(8,128)(2,1)S(1)}, bf16[256,1024]{1,0:T(8,128)(2,1)}, u32[]{:S(2)}) copy-start(bf16[256,1024]{1,0:T(8,128)(2,1)} %q_ref.1) | copy-start | bytes 1572868
  4.7 1.6 %copy-start.1 = (s32[2]{0:T(128)S(1)}, s32[2]{0:T(128)}, u32[]{:S(2)}) copy-start(s32[2]{0:T(128)} %off_ref.1) | copy-start | bytes 28
  4.7 1.6 %copy-start.2 = (s32[2]{0:T(128)S(1)}, s32[2]{0:T(128)}, u32[]{:S(2)}) copy-start(s32[2]{0:T(128)} %len_ref.1) | copy-start | bytes 28
  4.7 1.6 %copy-start.3 = (s32[128]{0:T(128)S(1)}, s32[128]{0:T(128)}, u32[]{:S(2)}) copy-start(s32[128]{0:T(128)} %storage_ref.1) | copy-start | bytes 1540
